TPU v7x, 32 devices: a whole 2x2x4 slice. The times are simulated.
32 devices in a mesh: gr: 8 (over y, x, core), gc: 4 (over z).
Axes of the slice: x: 2, y: 2, z: 4, core: 2. Of those that a mesh axis runs over, the one named last changes fastest.
Arguments:
- child_rows: float32 [4096, 12288], P('gr', 'gc'), may hold values from -1.5 to 1.5
- row_map: int32 [4096], P('gr'), may hold values from 0 to 4095, as said below
- stair: int32 [32], replicated, may hold values from 0 to 896, as said below
Outputs:
- factor: float32 [1024, 12288], P('gr', 'gc')
- projected: float32 [4096, 12288], P('gr', 'gc')
Inputs may be any that keep to these rules, and one draw needn't show every extreme that they name: row_map is a permutation of 0 to 4095. Of the 512 rows of one index of gr, at most 176 go to the rows of any one index of gr (row_map // 512), and some index of gr sends exactly 176 to one index. stair is nondecreasing and a multiple of 128; the first quarter of the blocks is 0 and the last block holds 896.
All inputs are finite; a program needn't handle non-finite values.
Results may differ from a plain program's by a relative error of at most 0.0003.
Values sent between devices are 32-bit elements; how exact they have to be, the bound alone decides.
No kernel may reach another device: no remote copies, remote signals or barrier semaphores. Data moves between devices by JAX's collectives and lax.ppermute only.
A program may use at most 128 MiB of HBM per device.

v0:
```python
import jax
import jax.numpy as jnp
from jax import lax
from jax.sharding import PartitionSpec as P

PANEL = 512
NPANEL = 2
STAIR_BLOCK = 128


def spread(value, axis, source):
    kept = jnp.where(lax.axis_index(axis) == source, value, 0).astype(value.dtype)
    return lax.psum(kept, axis)


def pack_rows(values, targets, groups):
    rows_dev = values.shape[0]
    base_rows = 3 * rows_dev // (4 * groups)
    capacity = rows_dev - base_rows * (groups - 1)
    target_dev = targets // rows_dev
    target_row = targets % rows_dev
    onehot = (target_dev[:, None] == jnp.arange(groups, dtype=jnp.int32)[None, :]).astype(jnp.int32)
    rank_within = jnp.sum((jnp.cumsum(onehot, axis=0) - onehot) * onehot, axis=1)
    buffer_index = target_dev * capacity + rank_within
    source_row = (
        jnp.full((groups * capacity,), rows_dev, jnp.int32)
        .at[buffer_index]
        .set(jnp.arange(rows_dev, dtype=jnp.int32))
    )
    sent_rows = jnp.take(values, source_row, axis=0, mode="fill", fill_value=0.0)
    sent_slots = (
        jnp.full((groups * capacity,), rows_dev, jnp.int32).at[buffer_index].set(target_row)
    )
    return (
        sent_rows.reshape(groups, capacity, values.shape[1]),
        sent_slots.reshape(groups, capacity),
    )


def place_rows(recv_rows, recv_slots, rows_dev):
    flat_rows = recv_rows.reshape(-1, recv_rows.shape[-1])
    flat_slots = recv_slots.reshape(-1)
    where_from = (
        jnp.zeros((rows_dev,), jnp.int32)
        .at[flat_slots]
        .set(jnp.arange(flat_slots.shape[0], dtype=jnp.int32), mode="drop")
    )
    return jnp.take(flat_rows, where_from, axis=0)


def matmul(left, right):
    return jnp.dot(left, right, precision=lax.Precision.HIGHEST, preferred_element_type=jnp.float32)


def shards(child_rows, row_map, stair):
    groups = lax.axis_size("gr")
    rows_dev, cols_dev = child_rows.shape
    columns = lax.axis_index("gc") * cols_dev + jnp.arange(cols_dev, dtype=jnp.int32)
    sent_rows, sent_slots = pack_rows(child_rows, row_map, groups)
    recv_rows, recv_slots = (
        lax.all_to_all(sent_rows, "gr", split_axis=0, concat_axis=0, tiled=True),
        lax.all_to_all(sent_slots, "gr", split_axis=0, concat_axis=0, tiled=True),
    )
    front_work = place_rows(recv_rows, recv_slots, rows_dev)
    own_rows = lax.axis_index("gr") * rows_dev + jnp.arange(rows_dev, dtype=jnp.int32)
    limits = jnp.take(stair, own_rows // STAIR_BLOCK)
    front_work = jnp.where(
        columns[None, :] >= limits[:, None], front_work, jnp.zeros_like(front_work)
    )
    blocks = []
    for step in range(NPANEL):
        panel_block = spread(front_work[:, step * PANEL : (step + 1) * PANEL], "gc", 0)
        gram_one = lax.psum(matmul(panel_block.T, panel_block), "gr")
        lower_one = jnp.linalg.cholesky(gram_one)
        basis_cols = jax.scipy.linalg.solve_triangular(lower_one, panel_block.T, lower=True).T
        coupling = lax.psum(matmul(basis_cols.T, front_work), "gr")
        front_work = front_work - matmul(basis_cols, coupling)
        blocks.append(coupling)
    stacked = jnp.concatenate(blocks, axis=0)
    share_rows = stacked.shape[0] // groups
    factor = lax.dynamic_slice_in_dim(stacked, lax.axis_index("gr") * share_rows, share_rows, 0)
    return (factor, front_work)


def solution(mesh):
    placed = (P("gr", "gc"), P("gr"), P())
    return jax.shard_map(
        shards,
        mesh=mesh,
        in_specs=placed,
        out_specs=(P("gr", "gc"), P("gr", "gc")),
        check_vma=False,
    )
```

profile of v0, /device:TPU:26, one launch (start us, length us, event | category | flops | bytes accessed | tf_op | source)
XLA Modules:
  0.0 1048.0 jit_solution(15688099573969738617)
XLA Ops:
  9.4 2.5 scatter_custom_fusion
  12.5 4.3 all-to-all-start
  16.8 2.4 scatter_custom_fusion.2
  19.4 19.7 %gather_fusion = f32[1408,3072]{1,0:T(8,128)} fusion(f32[512,3072]{1,0:T(8,128)} %param.6, s32[2048]{0:T(1024)S(1)} %pad_clamp_fusion), kind=kCustom, calls=%fused_computation | custom fusion | bytes 34608640 | tf_op jit(solution)/shard_map/jit(_take)/gather | solution.py:30
  39.1 12.2 %broadcast_select_fusion = f32[8,176,3072]{2,1,0:T(8,128)} fusion(f32[8,176,3072]{2,1,0:T(8,128)} %bitcast.150, pred[8,176]{1,0:T(8,128)(4,1)S(1)} %broadcast_in_dim.53), kind=kLoop, calls=%fused_computation.11 | loop fusion | flops 4325376 | bytes 34604416 | tf_op jit(solution)/shard_map/jit(_take)/select_n | solution.py:30
  51.3 5.9 all-to-all-start.1
  58.5 4.2 compare_select_fusion.3
  63.5 15.3 %select_select_fusion.3 = s32[512]{0:T(512)S(1)} fusion(pred[512]{0:T(512)(128)(4,1)S(1)} %get-tuple-element.98, pred[512]{0:T(512)(128)(4,1)S(1)} %get-tuple-element.99, pred[512]{0:T(512)(128)(4,1)S(1)} %get-tuple-element.100, pred[512]{0:T(512)(128)(4,1)S(1)} %get-tuple-element.101, pred[512]{0:T(512)(128)(4,1)S(1)} %get-tuple-element.102, ...), kind=kLoop, calls=%fused_computation.190 | loop fusion | flops 24576 | bytes 17000 | tf_op jit(solution)/shard_map/jit(_take)/select_n | solution.py:66
  79.0 7.9 scatter_custom_fusion.1
  86.9 158.4 %all-to-all-done.1 = f32[8,176,3072]{2,1,0:T(8,128)} async-done(((f32[8,176,3072]{2,1,0:T(8,128)}), f32[8,176,3072]{2,1,0:T(8,128)}, u32[]{:S(2)}, u32[]{:S(2)}) %all-to-all-start.1) | async-done | bytes 17301536 | tf_op jit(solution)/shard_map/all_to_all | solution.py:61
  245.3 13.2 %gather_fusion.1 = f32[512,3072]{1,0:T(8,128)} fusion(f32[1408,3072]{1,0:T(8,128)} %bitcast.37, s32[1024]{0:T(1024)S(1)} %pad_clamp_fusion.1), kind=kCustom, calls=%fused_computation.1 | custom fusion | bytes 12584960 | tf_op jit(solution)/shard_map/jit(_take)/gather | solution.py:48
  258.5 4.2 select_select_fusion
  262.7 2.7 copy-done.1
  266.6 50.5 %all-reduce.8.cloned.1.call-done = f32[512,512]{1,0:T(8,128)} async-done(((f32[512,512]{1,0:T(8,128)}), f32[512,512]{1,0:T(8,128)}) %all-reduce.8.cloned.1.call-update) | async-done | bytes 1048592 | tf_op jit(solution)/shard_map/psum | solution.py:13
  317.1 4.4 fusion.85
  322.1 56.1 %all-reduce.10.cloned.1.call-done = f32[512,512]{0,1:T(8,128)} async-done(((f32[512,512]{0,1:T(8,128)}), f32[512,512]{0,1:T(8,128)}) %all-reduce.10.cloned.1.call-update) | async-done | bytes 1048592 | tf_op jit(solution)/shard_map/psum | solution.py:73
  378.3 1.6 copy.10
  381.3 11.7 %cholesky.286 = f32[128,128]{1,0:T(8,128)S(1)} custom-call(f32[128,128]{1,0:T(8,128)S(1)} %cholesky.426), custom_call_target="Cholesky" | custom-call | tf_op jit(solution)/shard_map/jit(cholesky)/cholesky | solution.py:74
  393.2 9.8 custom-call.27
  403.7 11.7 %cholesky.305 = f32[128,128]{1,0:T(8,128)S(1)} custom-call(f32[128,128]{1,0:T(8,128)S(1)} %cholesky.430), custom_call_target="Cholesky" | custom-call | tf_op jit(solution)/shard_map/jit(cholesky)/cholesky | solution.py:74
  415.4 10.0 custom-call.28
  426.1 11.7 %cholesky.326 = f32[128,128]{1,0:T(8,128)S(1)} custom-call(f32[128,128]{1,0:T(8,128)S(1)} %cholesky.435), custom_call_target="Cholesky" | custom-call | tf_op jit(solution)/shard_map/jit(cholesky)/cholesky | solution.py:74
  437.8 9.8 custom-call.29
  448.2 11.7 %cholesky.343 = f32[128,128]{1,0:T(8,128)S(1)} custom-call(f32[128,128]{1,0:T(8,128)S(1)} %convolution_subtract_fusion.13), custom_call_target="Cholesky" | custom-call | tf_op jit(solution)/shard_map/jit(cholesky)/cholesky | solution.py:74
  465.7 8.5 while.4
  474.2 39.3 %custom-call.30 = f32[4,128,128]{1,2,0:T(8,128)S(1)} custom-call(f32[4,128,128]{2,1,0:T(8,128)S(1)} %get-tuple-element.18), custom_call_target="InvertDiagBlocksLowerTriangular" | custom-call | tf_op jit(solution)/shard_map/jit(_solve_triangular)/triangular_solve | solution.py:75
  516.4 1.5 convolution_subtract_fusion.7
  518.3 13.6 %fusion.14 = f32[512,3072]{1,0:T(8,128)} fusion(f32[512,3072]{1,0:T(8,128)} %copy-done.1, f32[128,512]{1,0:T(8,128)S(1)} %fusion.47, f32[128,512]{1,0:T(8,128)S(1)} %fusion.48, f32[128,512]{1,0:T(8,128)S(1)} %fusion.50, f32[128,512]{1,0:T(8,128)S(1)} %fusion.24), kind=kOutput, calls=%fused_computation.54 | convolution fusion | flops 9664462848 | bytes 13631488 | tf_op jit(solution)/shard_map/dot_general | solution.py:52
  532.0 104.3 %all-reduce.12.cloned.1.call-done = f32[512,3072]{1,0:T(8,128)} async-done(((f32[512,3072]{1,0:T(8,128)}), f32[512,3072]{1,0:T(8,128)}) %all-reduce.12.cloned.1.call-update) | async-done | bytes 6291472 | tf_op jit(solution)/shard_map/psum | solution.py:76
  636.3 12.9 %convolution_subtract_fusion.1 = f32[512,3072]{1,0:T(8,128)S(1)} fusion(f32[512,3072]{1,0:T(8,128)} %copy-done.1, f32[512,3072]{1,0:T(8,128)} %all-reduce.12.cloned.1.call-done, f32[128,512]{1,0:T(8,128)S(1)} %fusion.47, f32[128,512]{1,0:T(8,128)S(1)} %fusion.48, f32[128,512]{1,0:T(8,128)S(1)} %fusion.50, f32[128,512]{1,0:T(8,128)S(1)} %fusion.24), kind=kOutput, calls=%fused_computation.14 | convolution fusion | flops 9666035712 | bytes 19922944 | tf_op jit(solution)/shard_map/dot_general | solution.py:52
  649.2 2.7 copy-done
  653.1 50.5 %all-reduce.14.cloned.1.call-done = f32[512,512]{1,0:T(8,128)} async-done(((f32[512,512]{1,0:T(8,128)}), f32[512,512]{1,0:T(8,128)}) %all-reduce.14.cloned.1.call-update) | async-done | bytes 1048592 | tf_op jit(solution)/shard_map/psum | solution.py:13
  703.6 4.5 fusion.86
  708.3 56.5 %all-reduce.16.cloned.1.call-done = f32[512,512]{0,1:T(8,128)} async-done(((f32[512,512]{0,1:T(8,128)}), f32[512,512]{0,1:T(8,128)}) %all-reduce.16.cloned.1.call-update) | async-done | bytes 1048592 | tf_op jit(solution)/shard_map/psum | solution.py:73
  764.9 1.6 copy.12
  767.9 11.7 %cholesky.358 = f32[128,128]{1,0:T(8,128)S(1)} custom-call(f32[128,128]{1,0:T(8,128)S(1)} %cholesky.439), custom_call_target="Cholesky" | custom-call | tf_op jit(solution)/shard_map/jit(cholesky)/cholesky | solution.py:74
  779.8 9.8 custom-call.31
  790.3 11.7 %cholesky.377 = f32[128,128]{1,0:T(8,128)S(1)} custom-call(f32[128,128]{1,0:T(8,128)S(1)} %cholesky.443), custom_call_target="Cholesky" | custom-call | tf_op jit(solution)/shard_map/jit(cholesky)/cholesky | solution.py:74
  802.0 10.0 custom-call.32
  812.7 11.7 %cholesky.398 = f32[128,128]{1,0:T(8,128)S(1)} custom-call(f32[128,128]{1,0:T(8,128)S(1)} %cholesky.448), custom_call_target="Cholesky" | custom-call | tf_op jit(solution)/shard_map/jit(cholesky)/cholesky | solution.py:74
  824.4 9.8 custom-call.33
  834.9 11.7 %cholesky.415 = f32[128,128]{1,0:T(8,128)S(1)} custom-call(f32[128,128]{1,0:T(8,128)S(1)} %convolution_subtract_fusion.12), custom_call_target="Cholesky" | custom-call | tf_op jit(solution)/shard_map/jit(cholesky)/cholesky | solution.py:74
  852.4 8.5 while.5
  860.8 39.3 %custom-call.34 = f32[4,128,128]{1,2,0:T(8,128)S(1)} custom-call(f32[4,128,128]{2,1,0:T(8,128)S(1)} %get-tuple-element.19), custom_call_target="InvertDiagBlocksLowerTriangular" | custom-call | tf_op jit(solution)/shard_map/jit(_solve_triangular)/triangular_solve | solution.py:75
  904.9 13.6 %fusion.13 = f32[512,3072]{1,0:T(8,128)} fusion(f32[512,3072]{1,0:T(8,128)} %copy-done, f32[128,512]{1,0:T(8,128)S(1)} %fusion.41, f32[128,512]{1,0:T(8,128)S(1)} %fusion.42, f32[128,512]{1,0:T(8,128)S(1)} %fusion.44, f32[128,512]{1,0:T(8,128)S(1)} %fusion.21), kind=kOutput, calls=%fused_computation.53 | convolution fusion | flops 9664462848 | bytes 13631488 | tf_op jit(solution)/shard_map/dot_general | solution.py:52
  918.6 104.3 %all-reduce.18.cloned.1.call-done = f32[512,3072]{1,0:T(8,128)} async-done(((f32[512,3072]{1,0:T(8,128)}), f32[512,3072]{1,0:T(8,128)}) %all-reduce.18.cloned.1.call-update) | async-done | bytes 6291472 | tf_op jit(solution)/shard_map/psum | solution.py:76
  1022.9 15.2 %convolution_subtract_fusion = f32[512,3072]{1,0:T(8,128)} fusion(f32[512,3072]{1,0:T(8,128)} %copy-done, f32[512,3072]{1,0:T(8,128)} %all-reduce.18.cloned.1.call-done, f32[128,512]{1,0:T(8,128)S(1)} %fusion.41, f32[128,512]{1,0:T(8,128)S(1)} %fusion.42, f32[128,512]{1,0:T(8,128)S(1)} %fusion.44, f32[128,512]{1,0:T(8,128)S(1)} %fusion.21), kind=kOutput, calls=%fused_computation.13 | convolution fusion | flops 9666035712 | bytes 19922944 | tf_op jit(solution)/shard_map/dot_general | solution.py:52
  1038.2 2.8 fusion
  (143 shorter events, 46.6 us)
Async XLA Ops:
  12.5 38.8 %all-to-all-start = ((s32[8,1,176]{2,1,0:T(1,128)}), s32[8,1,176]{2,1,0:T(1,128)S(1)}, u32[]{:S(2)}, u32[]{:S(2)}) async-start(s32[8,1,176]{2,1,0:T(1,128)} %all_to_all.9), calls=%async_computation | async-start | bytes 16384 | tf_op jit(solution)/shard_map/all_to_all | solution.py:62
  51.3 6.5 copy-start.5
  51.3 194.0 %all-to-all-start.1 = ((f32[8,176,3072]{2,1,0:T(8,128)}), f32[8,176,3072]{2,1,0:T(8,128)}, u32[]{:S(2)}, u32[]{:S(2)}) async-start(f32[8,176,3072]{2,1,0:T(8,128)} %broadcast_select_fusion), calls=%async_computation.1 | async-start | bytes 34603008 | tf_op jit(solution)/shard_map/all_to_all | solution.py:61
  57.3 259.9 %all-reduce.8.cloned.1.call-start = ((), (), s32[]{:S(2)}) async-start(), calls=%async_computation.2 | async-start | bytes 2097152 | tf_op jit(solution)/shard_map/psum | solution.py:13
  262.7 2.7 copy-start.1
  266.5 111.7 %all-reduce.10.cloned.1.call-start = ((), (), s32[]{:S(2)}) async-start(), calls=%async_computation.3 | async-start | bytes 2097152 | tf_op jit(solution)/shard_map/psum | solution.py:73
  321.5 314.8 %all-reduce.12.cloned.1.call-start = ((), (), s32[]{:S(2)}) async-start(), calls=%async_computation.4 | async-start | bytes 12582912 | tf_op jit(solution)/shard_map/psum | solution.py:76
  322.1 191.4 %copy-start.3 = (f32[512,512]{1,0:T(8,128)S(1)}, f32[512,512]{1,0:T(8,128)}, u32[]{:S(2)}) copy-start(f32[512,512]{1,0:T(8,128)} %all-reduce.8.cloned.1.call-done) | copy-start | bytes 3145732
  532.0 171.6 %all-reduce.14.cloned.1.call-start = ((), (), s32[]{:S(2)}) async-start(), calls=%async_computation.5 | async-start | bytes 2097152 | tf_op jit(solution)/shard_map/psum | solution.py:13
  649.2 2.7 copy-start
  653.0 111.8 %all-reduce.16.cloned.1.call-start = ((), (), s32[]{:S(2)}) async-start(), calls=%async_computation.6 | async-start | bytes 2097152 | tf_op jit(solution)/shard_map/psum | solution.py:73
  708.1 314.8 %all-reduce.18.cloned.1.call-start = ((), (), s32[]{:S(2)}) async-start(), calls=%async_computation.7 | async-start | bytes 12582912 | tf_op jit(solution)/shard_map/psum | solution.py:76
  708.3 191.8 %copy-start.4 = (f32[512,512]{1,0:T(8,128)S(1)}, f32[512,512]{1,0:T(8,128)}, u32[]{:S(2)}) copy-start(f32[512,512]{1,0:T(8,128)} %all-reduce.14.cloned.1.call-done) | copy-start | bytes 3145732
  1022.9 15.2 %copy-start.2 = (f32[512,3072]{1,0:T(8,128)S(1)}, f32[512,3072]{1,0:T(8,128)}, u32[]{:S(2)}) copy-start(f32[512,3072]{1,0:T(8,128)} %all-reduce.18.cloned.1.call-done) | copy-start | bytes 18874372
Sparse Core Ops, SparseCore 0:
  266.7 50.4 all-reduce.7
  321.7 56.5 all-reduce.9
  532.1 104.1 all-reduce.11
  653.1 50.3 all-reduce.13
  708.2 56.5 all-reduce.15
  918.7 104.1 all-reduce.17
where the time goes:
time: 1060 us; the launch traced here: 1050 us
  waiting for transfers between devices  581 us (55%)
  other arithmetic  285 us (27%)
  matrix products  77.5 us (7%)
  local copies, waits for them, and re-layouts  73.8 us (7%)
  between operations  20 us (2%)
  starting transfers between devices  11.1 us (1%)
    psum x2, waiting for transfers between devices, shards(): coupling = lax.psum(matmul(basis_cols.T, front_work), 'gr')  209 us
    another operation x30, other arithmetic, shards(): lower_one = jnp.linalg.cholesky(gram_one)  158 us
    all_to_all x1, waiting for transfers between devices, shards(): lax.all_to_all(sent_rows, 'gr', split_axis=0, concat_axis=0, tiled=True)  158 us
    psum x2, waiting for transfers between devices, shards(): gram_one = lax.psum(matmul(panel_block.T, panel_block), 'gr')  113 us
    psum x2, waiting for transfers between devices, spread(): return lax.psum(kept, axis)  101 us
    another operation x5, other arithmetic, shards(): jax.scipy.linalg.solve_triangular(lower_one, panel_block.T, lower=True)  79.7 us
    dot_general x6, matrix products, matmul(): jnp.dot(left, right, precision=lax.Precision.HIGHEST, preferred_element_t...  64.3 us
  transfers between devices with their start and end apart: 8, of which 7 were waited for; matrix products, arithmetic and copies ran while one was open for 6% of the time, Pallas kernels for 0%

commit v1 on v0

v1 whole, which is shorter than its diff:
```python
import jax
import jax.numpy as jnp
from jax import lax
from jax.experimental import pallas as pl
from jax.experimental.pallas import tpu as pltpu
from jax.sharding import PartitionSpec as P

PANEL = 512
NPANEL = 2
STAIR_BLOCK = 128
EDGE = 128
HIGHEST = lax.Precision.HIGHEST
HIGH = lax.Precision.HIGH


def dot(left, right, dims, precision):
    return lax.dot_general(
        left, right, (dims, ((), ())), precision=precision, preferred_element_type=jnp.float32
    )


def eliminate(tiles):
    lane = lax.broadcasted_iota(jnp.int32, (8, EDGE), 1)
    sub = lax.broadcasted_iota(jnp.int32, (8, EDGE), 0)
    tiles = list(tiles)
    strips = len(tiles)
    for strip in range(strips):
        first = 8 * strip
        own = (lane >= first) & (lane < first + 8)
        mult = {
            t: [jnp.broadcast_to(tiles[t][:, first + s : first + s + 1], (8, EDGE)) for s in range(8)]
            for t in range(strip, strips)
        }
        small = [
            [jnp.broadcast_to(mult[strip][s][t : t + 1, :], (8, EDGE)) for s in range(t + 1)]
            for t in range(8)
        ]
        start = jnp.where(own, jnp.where(lane - first == sub, 1.0, 0.0), tiles[strip])
        rows = [jnp.broadcast_to(start[s : s + 1, :], (8, EDGE)) for s in range(8)]
        inv = [None] * 8
        low = [[None] * 8 for _ in range(8)]
        for s in range(8):
            inv[s] = 1.0 / small[s][s]
            for t in range(s + 1, 8):
                low[t][s] = small[t][s] * inv[s]
                for u in range(s + 1, t + 1):
                    small[t][u] = small[t][u] - low[t][s] * small[u][s]
            for t in range(s + 1, 8):
                rows[t] = rows[t] - low[t][s] * rows[s]
        back = [None] * 8
        for s in range(7, -1, -1):
            value = rows[s] * inv[s]
            for t in range(7, s, -1):
                value = value - low[t][s] * back[t]
            back[s] = value
        out, pivot = rows[7], small[7][7]
        for s in range(6, -1, -1):
            out = jnp.where(sub == s, rows[s], out)
            pivot = jnp.where(sub == s, small[s][s], pivot)
        tiles[strip] = out * lax.rsqrt(pivot)
        for t in range(strip + 1, strips):
            value = jnp.where(own, 0.0, tiles[t])
            for s in range(8):
                value = value - mult[t][s] * back[s]
            tiles[t] = value
    return tiles


def inverse_factor_kernel(gram_ref, out_ref, work):
    size = gram_ref.shape[0]
    blocks = size // EDGE
    work[...] = gram_ref[...]
    out_ref[...] = jnp.zeros_like(out_ref)
    lower = lax.broadcasted_iota(jnp.int32, (EDGE, EDGE), 0) >= lax.broadcasted_iota(
        jnp.int32, (EDGE, EDGE), 1
    )

    @pl.loop(0, blocks)
    def _(k):
        at = pl.multiple_of(k * EDGE, EDGE)
        tiles = [
            work[pl.ds(pl.multiple_of(at + 8 * t, 8), 8), pl.ds(at, EDGE)] for t in range(EDGE // 8)
        ]
        diag = jnp.where(lower, jnp.concatenate(eliminate(tiles), axis=0), 0.0)
        work[pl.ds(at, EDGE), :] = dot(diag, work[pl.ds(at, EDGE), :], ((1,), (0,)), HIGHEST)
        work[pl.ds(at, EDGE), pl.ds(at, EDGE)] = diag

        @pl.loop(k + 1, blocks)
        def _(i):
            below = pl.multiple_of(i * EDGE, EDGE)
            coeff = work[pl.ds(at, EDGE), pl.ds(below, EDGE)]
            work[pl.ds(below, EDGE), pl.ds(at, EDGE)] = jnp.zeros((EDGE, EDGE), jnp.float32)
            work[pl.ds(below, EDGE), :] -= dot(coeff, work[pl.ds(at, EDGE), :], ((0,), (0,)), HIGHEST)

        @pl.loop(0, k + 1)
        def _(j):
            left = pl.multiple_of(j * EDGE, EDGE)
            out_ref[pl.ds(at, EDGE), pl.ds(left, EDGE)] = work[pl.ds(at, EDGE), pl.ds(left, EDGE)]


def inverse_factor(gram):
    size = gram.shape[0]
    return pl.pallas_call(
        inverse_factor_kernel,
        out_shape=jax.ShapeDtypeStruct((size, size), jnp.float32),
        in_specs=[pl.BlockSpec(memory_space=pltpu.VMEM)],
        out_specs=pl.BlockSpec(memory_space=pltpu.VMEM),
        scratch_shapes=[pltpu.VMEM((size, size), jnp.float32)],
        compiler_params=pltpu.CompilerParams(vmem_limit_bytes=40 * 2**20),
        cost_estimate=pl.CostEstimate(
            flops=6 * 2 * size**3, bytes_accessed=8 * size * size, transcendentals=size
        ),
        name="inverse_factor",
    )(gram)


def pick(where_to, count):
    rows = lax.broadcasted_iota(jnp.int32, (count, where_to.shape[1]), 0)
    return jnp.where(rows == where_to, 1.0, 0.0).astype(jnp.bfloat16)


def move(matrix, values):
    high = values.astype(jnp.bfloat16)
    rest = (values - high.astype(jnp.float32)).astype(jnp.bfloat16)
    dims = ((1,), (0,))
    return dot(matrix, high, dims, None) + dot(matrix, rest, dims, None)


def reorder_kernel(to_ref, in_ref, out_ref, matrix):
    @pl.when(pl.program_id(0) == 0)
    def _():
        matrix[...] = pick(to_ref[...], matrix.shape[0])

    out_ref[...] = move(matrix[...], in_ref[...])


def block_width(width):
    for block in (384, 256, 128):
        if width % block == 0:
            return block
    return width


def reorder(values, where_to):
    count, width = values.shape
    block = block_width(width)
    return pl.pallas_call(
        reorder_kernel,
        grid=(width // block,),
        out_shape=jax.ShapeDtypeStruct((count, width), jnp.float32),
        in_specs=[
            pl.BlockSpec((1, count), lambda j: (0, 0)),
            pl.BlockSpec((count, block), lambda j: (0, j)),
        ],
        out_specs=pl.BlockSpec((count, block), lambda j: (0, j)),
        scratch_shapes=[pltpu.VMEM((count, count), jnp.bfloat16)],
        compiler_params=pltpu.CompilerParams(vmem_limit_bytes=40 * 2**20),
        cost_estimate=pl.CostEstimate(
            flops=4 * count * count * width, bytes_accessed=8 * count * width, transcendentals=0
        ),
        name="reorder",
    )(where_to.reshape(1, count), values)


def place_kernel(to_ref, limit_ref, direct_ref, other_ref, out_ref, matrix):
    block = pl.program_id(0)

    @pl.when(block == 0)
    def _():
        matrix[...] = pick(to_ref[...], matrix.shape[0])

    count = direct_ref.shape[0]
    value = move(matrix[:, :count], direct_ref[...]) + move(matrix[:, count:], other_ref[...])
    column = lax.broadcasted_iota(jnp.int32, value.shape, 1) + block * value.shape[1]
    out_ref[...] = jnp.where(column >= limit_ref[...], value, 0.0)


def place(direct, other, where_to, limits):
    rows = limits.shape[0]
    width = direct.shape[1]
    block = block_width(width)
    return pl.pallas_call(
        place_kernel,
        grid=(width // block,),
        out_shape=jax.ShapeDtypeStruct((rows, width), jnp.float32),
        in_specs=[
            pl.BlockSpec((1, rows), lambda j: (0, 0)),
            pl.BlockSpec((rows, 1), lambda j: (0, 0)),
            pl.BlockSpec((direct.shape[0], block), lambda j: (0, j)),
            pl.BlockSpec((other.shape[0], block), lambda j: (0, j)),
        ],
        out_specs=pl.BlockSpec((rows, block), lambda j: (0, j)),
        scratch_shapes=[pltpu.VMEM((rows, rows), jnp.bfloat16)],
        compiler_params=pltpu.CompilerParams(vmem_limit_bytes=40 * 2**20),
        cost_estimate=pl.CostEstimate(
            flops=4 * rows * rows * width, bytes_accessed=8 * rows * width, transcendentals=0
        ),
        name="place",
    )(where_to.reshape(1, rows), limits.reshape(rows, 1), direct, other)


def exchange_plan(row_map, groups, rows_dev, base):
    me = lax.axis_index("gr")
    other = rows_dev - groups * base
    every = lax.all_to_all(
        jnp.broadcast_to(row_map[None, :], (groups, rows_dev)), "gr", 0, 0, tiled=True
    )
    dest, slot = every // rows_dev, every % rows_dev
    at = jnp.arange(rows_dev, dtype=jnp.int32)
    before = (at[:, None] < at[None, :]).astype(jnp.bfloat16)
    group_ids = jnp.arange(groups, dtype=jnp.int32)
    onehot = dest[:, None, :] == group_ids[None, :, None]
    ahead = dot(
        onehot.reshape(groups * groups, rows_dev).astype(jnp.bfloat16), before, ((1,), (0,)), None
    ).reshape(groups, groups, rows_dev)
    rank = jnp.sum(jnp.where(onehot, ahead, 0.0), axis=1).astype(jnp.int32)
    late = rank >= base
    late_rank = dot(late.astype(jnp.bfloat16), before, ((1,), (0,)), None).astype(jnp.int32)
    sent = jnp.sum(onehot.astype(jnp.int32), axis=2) - base
    earlier = jnp.cumsum(sent, axis=0) - sent
    start = jnp.sum(jnp.where(onehot, earlier[:, :, None], 0), axis=1)
    turn = start + rank - base
    pack_to = jnp.where(late, groups * base + late_rank, dest * base + rank)
    pack_to = lax.dynamic_index_in_dim(pack_to, me, 0, keepdims=False)
    late_ids = jnp.arange(other, dtype=jnp.int32)
    chosen = late[:, None, :] & (late_rank[:, None, :] == late_ids[None, :, None])
    turn_to = jnp.sum(jnp.where(chosen, (dest * other + turn)[:, None, :], 0), axis=2).reshape(-1)
    arrival = jnp.where(late, groups * base + turn, group_ids[:, None] * base + rank)
    arrival = jnp.where(dest == me, arrival, -1).reshape(-1)
    place_to = jnp.sum(
        jnp.where(arrival[None, :] == at[:, None], slot.reshape(-1)[None, :], 0), axis=1
    )
    return pack_to, turn_to, place_to


def exchange_rows(values, row_map, limits):
    groups = lax.axis_size("gr")
    rows_dev, width = values.shape
    base = 3 * rows_dev // (4 * groups)
    other = rows_dev - groups * base
    part = width // groups
    pack_to, turn_to, place_to = exchange_plan(row_map, groups, rows_dev, base)
    packed = reorder(values, pack_to)
    direct = lax.all_to_all(
        packed[: groups * base].reshape(groups, base, width), "gr", 0, 0, tiled=True
    ).reshape(groups * base, width)
    split = packed[groups * base :].reshape(other, groups, part).transpose(1, 0, 2)
    split = lax.all_to_all(split, "gr", 0, 0, tiled=True).reshape(groups * other, part)
    split = reorder(split, turn_to).reshape(groups, other, part)
    split = lax.all_to_all(split, "gr", 0, 0, tiled=True)
    joined = split.transpose(1, 0, 2).reshape(other, width)
    return place(direct, joined, place_to, limits)


def bits_of(groups):
    count = groups.bit_length() - 1
    orders = (list(range(1, count)), list(range(count - 1, 0, -1)))
    me = lax.axis_index("gr")
    stages = []
    for one, two in zip(*orders):
        pairs = [(i, i ^ (1 << (two if i & 1 else one))) for i in range(groups)]
        mine = jnp.where(me & 1, (me >> two) & 1, (me >> one) & 1)
        stages.append((pairs, mine))
    return stages


def in_plane(pairs, planes, chosen):
    return [(a * planes + z, b * planes + z) for a, b in pairs for z in chosen]


def swap(value, groups):
    return lax.ppermute(value, "gr", [(i, i ^ 1) for i in range(groups)])


def reduce_parts(value, groups, planes, chosen):
    for pairs, mine in bits_of(groups):
        half = value.shape[0] // 2
        keep = lax.dynamic_slice_in_dim(value, mine * half, half, 0)
        give = lax.dynamic_slice_in_dim(value, (1 - mine) * half, half, 0)
        value = keep + lax.ppermute(give, ("gr", "gc"), in_plane(pairs, planes, chosen))
    return value


def join(value, came, mine):
    return jnp.where(
        mine == 0, jnp.concatenate([value, came], axis=0), jnp.concatenate([came, value], axis=0)
    )


def gather_parts(value, groups):
    for pairs, mine in reversed(bits_of(groups)):
        value = join(value, lax.ppermute(value, "gr", pairs), mine)
    return join(value, swap(value, groups), lax.axis_index("gr") & 1)


def from_first_plane(value, planes):
    me = lax.axis_index("gc")
    step = planes // 2
    while step:
        pairs = [(i, i + step) for i in range(0, planes, 2 * step)]
        came = lax.ppermute(value, "gc", pairs)
        value = jnp.where(me % (2 * step) == step, came, value)
        step //= 2
    return value


def shards(child_rows, row_map, stair):
    groups, planes = lax.axis_size("gr"), lax.axis_size("gc")
    me, plane = lax.axis_index("gr"), lax.axis_index("gc")
    core = me & 1
    rows_dev, cols_dev = child_rows.shape
    panels = NPANEL * PANEL
    half = cols_dev // 2
    columns = jnp.arange(cols_dev, dtype=jnp.int32)
    blocks = jnp.arange(stair.shape[0], dtype=jnp.int32)
    child_limits = jnp.sum(
        jnp.where((row_map // STAIR_BLOCK)[:, None] == blocks[None, :], stair[None, :], 0), axis=1
    )
    child_limits = child_limits - plane * cols_dev
    own_blocks = rows_dev // STAIR_BLOCK
    limits = jnp.repeat(
        lax.dynamic_slice_in_dim(stair, me * own_blocks, own_blocks, 0), STAIR_BLOCK
    )
    limits = limits - plane * cols_dev

    masked = jnp.where(columns[None, :] >= child_limits[:, None], child_rows, 0.0)
    panel = masked[:, :panels]
    both = jnp.concatenate([panel, swap(panel, groups)], axis=0)

    share = lax.dynamic_slice_in_dim(both, core * (panels // 2), panels // 2, 1)
    gram = dot(share, both, ((0,), (0,)), HIGHEST)
    gram = reduce_parts(gram, groups, planes, [0])
    gram = from_first_plane(gram, planes)
    gram = gather_parts(gram, groups)
    inverse = inverse_factor(gram)

    panel = from_first_plane(panel, planes)
    both = jnp.concatenate([panel, swap(panel, groups)], axis=0)
    mine = lax.dynamic_slice_in_dim(masked, core * half, half, 1)
    theirs = lax.dynamic_slice_in_dim(masked, (1 - core) * half, half, 1)
    share = jnp.concatenate([mine, swap(theirs, groups)], axis=0)
    product = dot(share, both, ((0,), (0,)), HIGH)
    product = reduce_parts(product, groups, planes, range(planes))
    coupling = dot(product, inverse, ((1,), (1,)), HIGHEST)
    coupling = gather_parts(coupling, groups)

    front = exchange_rows(child_rows, row_map, limits)
    own_panel = from_first_plane(front[:, :panels], planes)
    basis = dot(own_panel, inverse, ((1,), (1,)), HIGHEST)
    projected = front - dot(basis, coupling, ((1,), (1,)), HIGH)
    share_rows = panels // groups
    factor = lax.dynamic_slice_in_dim(coupling, me * share_rows, share_rows, 1).T
    return (factor, projected)


def solution(mesh):
    placed = (P("gr", "gc"), P("gr"), P())
    return jax.shard_map(
        shards,
        mesh=mesh,
        in_specs=placed,
        out_specs=(P("gr", "gc"), P("gr", "gc")),
        check_vma=False,
    )
```

time: 1060 us -> 590 us (0.56)
  waiting for transfers between devices: 581 us -> 322 us
  other arithmetic: 285 us -> 52.4 us
  Pallas kernels: 0 us -> 83 us
  local copies, waits for them, and re-layouts: 73.8 us -> 30 us
  starting transfers between devices: 11.1 us -> 37.6 us
  matrix products: 77.5 us -> 55.2 us
  between operations: 20 us -> 1.4 us
    psum x6 -> x0, waiting for transfers between devices: 422 us -> none  [the longest x2 209 us: shards(): coupling = lax.psum(matmul(basis_cols.T, front_work), 'gr')]
    ppermute x0 -> x19, waiting for transfers between devices: none -> 264 us  [the longest x6 194 us: from_first_plane(): came = lax.ppermute(value, 'gc', pairs)]
    another operation x37 -> x1, other arithmetic: 239 us -> 0.03 us  [exchange_plan(): earlier = jnp.cumsum(sent, axis=0) - sent]
    all_to_all x2 -> x4, waiting for transfers between devices: 158 us -> 58 us  [the longest x1 40.7 us: exchange_plan(): lax.all_to_all(jnp.broadcast_to(row_map[None, :], (groups, rows_dev)), 'g...]
    pallas_call x0 -> x4, Pallas kernels: none -> 83 us  [the longest x1 63.8 us: inverse_factor(): pl.pallas_call(inverse_factor_kernel, out_shape=jax.ShapeDtypeStruct((siz...]
    gather x4 -> x0, local copies, waits for them, and re-layouts: 34.3 us -> none  [the longest x1 19.7 us: pack_rows(): jnp.take(values, source_row, axis=0, mode='fill', fill_value=0.0)]
    ppermute x0 -> x19, starting transfers between devices: none -> 18.3 us  [the longest x6 7.65 us: from_first_plane(): came = lax.ppermute(value, 'gc', pairs)]
    another operation x37 -> x0, local copies, waits for them, and re-layouts: 17.3 us -> none  [the longest x27 16.8 us: shards(): jax.scipy.linalg.solve_triangular(lower_one, panel_block.T, lower=True)]
  transfers between devices with their start and end apart: 8 -> 23, of which waited for: 7 -> 8; matrix products, arithmetic and copies ran while one was open for 6% -> 17% of each run, Pallas kernels for 0% -> 14%
where the time goes in v1:
time: 590 us; the launch traced here: 582 us
  waiting for transfers between devices  322 us (55%)
  Pallas kernels  83 us (14%)
  matrix products  55.2 us (9%)
  other arithmetic  52.4 us (9%)
  starting transfers between devices  37.6 us (6%)
  local copies, waits for them, and re-layouts  30 us (5%)
    ppermute x6, waiting for transfers between devices, from_first_plane(): came = lax.ppermute(value, 'gc', pairs)  194 us
    ppermute x4, waiting for transfers between devices, gather_parts(): value = join(value, lax.ppermute(value, 'gr', pairs), mine)  69.7 us
    pallas_call x1, Pallas kernels, inverse_factor(): pl.pallas_call(inverse_factor_kernel, out_shape=jax.ShapeDtypeStruct((siz...  63.8 us
    dot_general x7, matrix products, dot(): lax.dot_general(left, right, (dims, ((), ())), precision=precision, prefe...  55.2 us
    all_to_all x1, waiting for transfers between devices, exchange_plan(): lax.all_to_all(jnp.broadcast_to(row_map[None, :], (groups, rows_dev)), 'g...  40.7 us
    select_n x6, other arithmetic, join(): jnp.where(mine == 0, jnp.concatenate([value, came], axis=0), jnp.concaten...  29.5 us
    all_to_all x1, waiting for transfers between devices, exchange_rows(): lax.all_to_all(packed[:groups * base].reshape(groups, base, width), 'gr',...  17 us
  transfers between devices with their start and end apart: 23, of which 8 were waited for; matrix products, arithmetic and copies ran while one was open for 17% of the time, Pallas kernels for 14%

profile of v1, /device:TPU:26, one launch (start us, length us, event | category | flops | bytes accessed | tf_op | source)
XLA Modules:
  0.0 581.6 jit_solution(11697033956762729905)
XLA Ops:
  2.1 3.7 fusion.4
  5.8 2.7 copy-done.3
  8.7 2.0 collective-permute-start.1
  10.7 3.5 broadcast_select_fusion.1
  15.4 8.7 %fusion.5 = f32[512,1024]{1,0:T(8,128)S(1)} fusion(f32[512,1024]{1,0:T(8,128)} %collective-permute-done.6, f32[512,1024]{1,0:T(8,128)S(1)} %slice.16, s32[]{:T(128)S(6)} %select_n.257), kind=kOutput, calls=%fused_computation.14 | convolution fusion | flops 6444023808 | bytes 10485764 | tf_op jit(solution)/shard_map/dot_general | solution.py:17
  25.5 1.7 collective-permute-start.7
  27.2 6.1 %constant_dynamic-slice_fusion.11 = (f32[512,1536]{1,0:T(8,128)}, f32[512,1536]{1,0:T(8,128)}) fusion(f32[512,3072]{1,0:T(8,128)} %copy-done.3, s32[]{:T(128)S(6)} %select_n.240, s32[]{:T(128)S(6)} %select_n.241), kind=kLoop, calls=%fused_computation.95 | loop fusion | bytes 12582920 | tf_op jit(solution)/shard_map/dynamic_slice | solution.py:339
  33.8 1.4 dynamic-slice_add_fusion.1
  35.9 73.9 %collective-permute-done.2 = f32[512,1024]{1,0:T(8,128)} collective-permute-done((f32[512,1024]{1,0:T(8,128)}, f32[512,1024]{1,0:T(8,128)}, u32[]{:S(2)}, u32[]{:S(2)}) %collective-permute-start.2) | collective-permute-done | bytes 2097184 | tf_op jit(solution)/shard_map/ppermute | solution.py:301
  109.8 3.5 broadcast_select_fusion.2
  115.1 1.5 collective-permute-start.10
  116.6 28.0 %collective-permute-done.10 = f32[128,1024]{1,0:T(8,128)} collective-permute-done((f32[128,1024]{1,0:T(8,128)}, f32[128,1024]{1,0:T(8,128)}, u32[]{:S(2)}, u32[]{:S(2)}) %collective-permute-start.10) | collective-permute-done | bytes 524320 | tf_op jit(solution)/shard_map/ppermute | solution.py:301
  144.6 1.9 broadcast_select_fusion.4
  146.5 1.5 collective-permute-start.11
  148.0 14.8 %fusion = f32[1536,1024]{1,0:T(8,128)S(1)} fusion(f32[512,1536]{1,0:T(8,128)} %collective-permute-done, f32[512,1536]{1,0:T(8,128)S(1)} %copy-done.11, f32[512,1024]{1,0:T(8,128)} %collective-permute-done.3, f32[512,1024]{1,0:T(8,128)} %broadcast_select_fusion.2), kind=kOutput, calls=%fused_computation.3 | convolution fusion | flops 9666297856 | bytes 16777216 | tf_op jit(solution)/shard_map/dot_general | solution.py:17
  162.9 2.1 constant_dynamic-slice_fusion.9
  165.0 1.5 copy-done.10
  167.0 1.7 maximum_select_fusion.5
  168.8 1.6 collective-permute-start.12
  171.0 3.8 all-to-all-start
  174.7 40.7 %all-to-all-done = s32[8,1,512]{2,1,0:T(1,128)S(1)} async-done(((s32[8,1,512]{2,1,0:T(1,128)}), s32[8,1,512]{2,1,0:T(1,128)S(1)}, u32[]{:S(2)}, u32[]{:S(2)}) %all-to-all-start) | async-done | bytes 16416 | tf_op jit(solution)/shard_map/all_to_all | solution.py:205
  215.7 3.4 maximum_select_fusion.4
  219.9 4.0 dynamic-slice_add_fusion
  223.9 1.5 constant_dynamic-slice_fusion.8
  227.5 6.7 %reorder.2 = f32[512,3072]{1,0:T(8,128)S(1)} custom-call(s32[1,512]{1,0:T(1,128)S(1)} %dynamic-slice_select_fusion.to_ref, f32[512,3072]{1,0:T(8,128)S(1)} %bitcast.56), custom_call_target="tpu_custom_call" | custom-call | flops 3221225472 | bytes 12582912 | tf_op jit(solution)/shard_map/reorder/pallas_call | solution.py:147
  234.3 1.4 copy.51
  235.7 1.6 copy-done.1
  237.3 4.3 all-to-all-start.2
  241.7 4.8 maximum_select_fusion.2.gram_ref
  246.5 63.8 %inverse_factor.1 = f32[1024,1024]{1,0:T(8,128)S(1)} custom-call(f32[1024,1024]{1,0:T(8,128)S(1)} %maximum_select_fusion.2.gram_ref), custom_call_target="tpu_custom_call" | custom-call | flops 12884901888 | bytes 8388608 | tf_op jit(solution)/shard_map/inverse_factor/pallas_call | solution.py:103
  310.4 7.9 %fusion.14 = f32[384,1024]{1,0:T(8,128)S(1)} fusion(f32[1024,1024]{1,0:T(8,128)S(1)} %inverse_factor.1, f32[384,1024]{1,0:T(8,128)} %collective-permute-done.5, f32[768,1024]{1,0:T(8,128)S(1)} %copy-done.5, s32[]{:T(128)S(6)} %select_n.250), kind=kOutput, calls=%fused_computation.30 | convolution fusion | flops 4832231424 | bytes 8912900 | tf_op jit(solution)/shard_map/dot_general | solution.py:17
  318.3 1.6 collective-permute-start.14
  320.4 3.5 reorder.3
  323.9 4.7 all-to-all-start.3
  328.6 20.1 %collective-permute-done.14 = f32[384,1024]{1,0:T(8,128)} collective-permute-done((f32[384,1024]{1,0:T(8,128)S(1)}, f32[384,1024]{1,0:T(8,128)}, u32[]{:S(2)}, u32[]{:S(2)}) %collective-permute-start.14) | collective-permute-done | bytes 1572896 | tf_op jit(solution)/shard_map/ppermute | solution.py:292
  348.7 3.6 maximum_select_fusion.3
  352.3 5.0 slice.17
  357.6 6.5 %all-to-all-start.1 = ((f32[8,48,3072]{2,1,0:T(8,128)}), f32[8,48,3072]{2,1,0:T(8,128)}, u32[]{:S(2)}, u32[]{:S(2)}) async-start(f32[8,48,3072]{2,1,0:T(8,128)} %bitcast.61), calls=%async_computation.1 | async-start | bytes 9437184 | tf_op jit(solution)/shard_map/all_to_all | solution.py:244
  364.0 49.6 %collective-permute-done.15 = f32[768,1024]{1,0:T(8,128)} collective-permute-done((f32[768,1024]{1,0:T(8,128)S(1)}, f32[768,1024]{1,0:T(8,128)}, u32[]{:S(2)}, u32[]{:S(2)}) %collective-permute-start.15) | collective-permute-done | bytes 3145760 | tf_op jit(solution)/shard_map/ppermute | solution.py:292
  413.7 5.4 maximum_select_fusion.1
  421.7 1.6 copy.30
  423.3 17.0 %all-to-all-done.1 = f32[8,48,3072]{2,1,0:T(8,128)} async-done(((f32[8,48,3072]{2,1,0:T(8,128)}), f32[8,48,3072]{2,1,0:T(8,128)}, u32[]{:S(2)}, u32[]{:S(2)}) %all-to-all-start.1) | async-done | bytes 4718624 | tf_op jit(solution)/shard_map/all_to_all | solution.py:244
  440.3 9.0 %place.1 = f32[512,3072]{1,0:T(8,128)S(1)} custom-call(s32[1,512]{1,0:T(1,128)S(1)} %bitcast.59, s32[512,1]{1,0:T(8,128)S(1)} %copy.26.limit_ref, f32[384,3072]{1,0:T(8,128)} %bitcast.7.direct_ref, f32[128,3072]{1,0:T(8,128)S(1)} %bitcast.57), custom_call_target="tpu_custom_call" | custom-call | flops 3221225472 | bytes 12582912 | tf_op jit(solution)/shard_map/place/pallas_call | solution.py:182
  453.3 92.3 %collective-permute-done.18 = f32[512,1024]{1,0:T(8,128)} collective-permute-done((f32[512,1024]{1,0:T(8,128)S(1)}, f32[512,1024]{1,0:T(8,128)}, u32[]{:S(2)}, u32[]{:S(2)}) %collective-permute-start.18) | collective-permute-done | bytes 2097184 | tf_op jit(solution)/shard_map/ppermute | solution.py:301
  545.6 10.4 %fusion.11 = f32[512,1024]{1,0:T(8,128)} fusion(f32[1024,1024]{1,0:T(8,128)} %copy-done.2, f32[512,1024]{1,0:T(8,128)} %collective-permute-done.18, f32[512,1024]{1,0:T(8,128)S(1)} %broadcast_select_fusion, pred[]{:T(512)S(6)} %eq.103), kind=kOutput, calls=%fused_computation.23 | convolution fusion | flops 6442975232 | bytes 10485761 | tf_op jit(solution)/shard_map/dot_general | solution.py:17
  556.0 10.4 %maximum_select_fusion = f32[3072,1024]{1,0:T(8,128)S(1)} fusion(f32[1536,1024]{1,0:T(8,128)} %collective-permute-done.16, f32[1536,1024]{1,0:T(8,128)} %maximum_select_fusion.1, pred[]{:T(512)S(6)} %eq.97), kind=kLoop, calls=%fused_computation | loop fusion | flops 9437184 | bytes 25165824 | tf_op jit(solution)/shard_map/jit(_where)/select_n | solution.py:285
  566.5 13.0 %convolution_subtract_fusion = f32[512,3072]{1,0:T(8,128)} fusion(f32[512,3072]{1,0:T(8,128)S(1)} %bitcast.54, f32[512,1024]{1,0:T(8,128)S(1)} %copy-done.8, f32[3072,1024]{1,0:T(8,128)S(1)} %maximum_select_fusion), kind=kOutput, calls=%fused_computation.13 | convolution fusion | flops 9665249280 | bytes 27262976 | tf_op jit(solution)/shard_map/dot_general | solution.py:17
  579.8 1.6 copy.27
  (98 shorter events, 19.2 us)
Async XLA Ops:
  5.8 2.7 copy-start.3
  8.7 2.0 collective-permute-start.1
  10.7 4.8 collective-permute-start.6
  14.1 95.7 %collective-permute-start.2 = (f32[512,1024]{1,0:T(8,128)}, f32[512,1024]{1,0:T(8,128)}, u32[]{:S(2)}, u32[]{:S(2)}) collective-permute-start(f32[512,1024]{1,0:T(8,128)} %broadcast_select_fusion.1), channel_id=1, source_target_pairs={{0,1},{2,3},{4,5},{6,7},{8,9},{10,11},{12,13},{14,15},{16,17},{18,... | collective-permute-start | bytes 6291464 | tf_op jit(solution)/shard_map/ppermute | solution.py:301
  24.1 1.3 copy-start.6
  25.5 8.2 %collective-permute-start.7 = (f32[256,1024]{1,0:T(8,128)S(1)}, f32[256,1024]{1,0:T(8,128)}, u32[]{:S(2)}, u32[]{:S(2)}) collective-permute-start(f32[256,1024]{1,0:T(8,128)S(1)} %constant_dynamic-slice_fusion.6), channel_id=1, source_target_pairs={{0,8},{4,20},{8,0},{12,28},{16,24},{20,4},{24,16},{28,12}} | collective-permute-start | bytes 3145736 | tf_op jit(solution)/shard_map/ppermute | solution.py:280
  27.2 6.6 %copy-start.7 = (f32[512,1024]{1,0:T(8,128)S(1)}, f32[512,1024]{1,0:T(8,128)}, u32[]{:S(2)}) copy-start(f32[512,1024]{1,0:T(8,128)} %copy-done.6) | copy-start | bytes 6291460
  33.3 114.7 %collective-permute-start = (f32[512,1536]{1,0:T(8,128)}, f32[512,1536]{1,0:T(8,128)}, u32[]{:S(2)}, u32[]{:S(2)}) collective-permute-start(f32[512,1536]{1,0:T(8,128)} %get-tuple-element.13), channel_id=1, source_target_pairs={{0,4},{4,0},{8,12},{12,8},{16,20},{20,16},{24,28},{28,24},{1,5},{5... | collective-permute-start | bytes 9437192 | tf_op jit(solution)/shard_map/ppermute | solution.py:272
  35.2 78.1 %collective-permute-start.8 = (f32[128,1024]{1,0:T(8,128)S(1)}, f32[128,1024]{1,0:T(8,128)S(1)}, u32[]{:S(2)}, u32[]{:S(2)}) collective-permute-start(f32[128,1024]{1,0:T(8,128)S(1)} %constant_dynamic-slice_fusion.5), channel_id=1, source_target_pairs={{0,16},{4,12},{8,24},{12,4},{16,0},{20,28},{24,8},{28,20}} | collective-permute-start | bytes 1572872 | tf_op jit(solution)/shard_map/ppermute | solution.py:280
  113.3 34.7 %collective-permute-start.3 = (f32[512,1024]{1,0:T(8,128)}, f32[512,1024]{1,0:T(8,128)}, u32[]{:S(2)}, u32[]{:S(2)}) collective-permute-start(f32[512,1024]{1,0:T(8,128)} %broadcast_select_fusion.2), channel_id=1, source_target_pairs={{0,4},{4,0},{8,12},{12,8},{16,20},{20,16},{24,28},{28,24},{1,5},{5... | collective-permute-start | bytes 6291464 | tf_op jit(solution)/shard_map/ppermute | solution.py:272
  113.4 34.6 %copy-start.11 = (f32[512,1536]{1,0:T(8,128)S(1)}, f32[512,1536]{1,0:T(8,128)}, u32[]{:S(2)}) copy-start(f32[512,1536]{1,0:T(8,128)} %get-tuple-element.12) | copy-start | bytes 9437188
  113.4 0.8 collective-permute-start.9
  115.1 29.5 %collective-permute-start.10 = (f32[128,1024]{1,0:T(8,128)}, f32[128,1024]{1,0:T(8,128)}, u32[]{:S(2)}, u32[]{:S(2)}) collective-permute-start(f32[128,1024]{1,0:T(8,128)} %broadcast_select_fusion.3), channel_id=1, source_target_pairs={{0,1},{2,3},{4,5},{6,7},{8,9},{10,11},{12,13},{14,15},{16,17},{18,... | collective-permute-start | bytes 1572872 | tf_op jit(solution)/shard_map/ppermute | solution.py:301
  146.5 20.5 %collective-permute-start.11 = (f32[128,1024]{1,0:T(8,128)}, f32[128,1024]{1,0:T(8,128)}, u32[]{:S(2)}, u32[]{:S(2)}) collective-permute-start(f32[128,1024]{1,0:T(8,128)} %broadcast_select_fusion.4), channel_id=1, source_target_pairs={{0,16},{4,12},{8,24},{12,4},{16,0},{20,28},{24,8},{28,20},{1,17},{... | collective-permute-start | bytes 1572872 | tf_op jit(solution)/shard_map/ppermute | solution.py:292
  162.8 3.7 copy-start.10
  162.8 7.5 %copy-start.12 = (s32[512]{0:T(512)S(1)}, s32[512]{0:T(512)}, u32[]{:S(2)}) copy-start(s32[512]{0:T(512)} %param.4) | copy-start | bytes 6148
  166.5 53.4 %collective-permute-start.4 = (f32[768,1024]{1,0:T(8,128)}, f32[768,1024]{1,0:T(8,128)}, u32[]{:S(2)}, u32[]{:S(2)}) collective-permute-start(f32[768,1024]{1,0:T(8,128)} %constant_dynamic-slice_fusion.9), channel_id=1, source_target_pairs={{0,8},{1,9},{2,10},{3,11},{4,20},{5,21},{6,22},{7,23},{8,0},{9,1},... | collective-permute-start | bytes 9437192 | tf_op jit(solution)/shard_map/ppermute | solution.py:280
  168.8 46.9 %collective-permute-start.12 = (f32[256,1024]{1,0:T(8,128)S(1)}, f32[256,1024]{1,0:T(8,128)}, u32[]{:S(2)}, u32[]{:S(2)}) collective-permute-start(f32[256,1024]{1,0:T(8,128)S(1)} %maximum_select_fusion.5), channel_id=1, source_target_pairs={{0,8},{4,20},{8,0},{12,28},{16,24},{20,4},{24,16},{28,12},{1,9},{5... | collective-permute-start | bytes 3145736 | tf_op jit(solution)/shard_map/ppermute | solution.py:292
  171.0 44.5 %all-to-all-start = ((s32[8,1,512]{2,1,0:T(1,128)}), s32[8,1,512]{2,1,0:T(1,128)S(1)}, u32[]{:S(2)}, u32[]{:S(2)}) async-start(s32[8,1,512]{2,1,0:T(1,128)} %broadcast_in_dim.88), calls=%async_computation | async-start | bytes 32768 | tf_op jit(solution)/shard_map/all_to_all | solution.py:205
  215.7 11.8 %slice-start.2 = ((s8[6291456]{0:T(1024)(128)(4,1)}), s8[2097152]{0:T(1024)(128)(4,1)S(1)}, s32[]{:S(2)}) async-start(s8[6291456]{0:T(1024)(128)(4,1)} %bitcast.55), calls=%async_computation.6 | async-start | bytes 4194304
  219.1 22.6 %collective-permute-start.13 = (f32[512,1024]{1,0:T(8,128)}, f32[512,1024]{1,0:T(8,128)}, u32[]{:S(2)}, u32[]{:S(2)}) collective-permute-start(f32[512,1024]{1,0:T(8,128)} %maximum_select_fusion.4), channel_id=1, source_target_pairs={{0,4},{4,0},{8,12},{12,8},{16,20},{20,16},{24,28},{28,24},{1,5},{5... | collective-permute-start | bytes 6291464 | tf_op jit(solution)/shard_map/ppermute | solution.py:272
  219.9 7.6 %slice-start.3 = ((s8[6291456]{0:T(1024)(128)(4,1)}), s8[4194304]{0:T(1024)(128)(4,1)S(1)}, s32[]{:S(2)}) async-start(s8[6291456]{0:T(1024)(128)(4,1)} %bitcast.55), calls=%async_computation.7 | async-start | bytes 8388608
  223.9 2.3 copy-start.4
  226.2 84.2 %collective-permute-start.5 = (f32[384,1024]{1,0:T(8,128)}, f32[384,1024]{1,0:T(8,128)}, u32[]{:S(2)}, u32[]{:S(2)}) collective-permute-start(f32[384,1024]{1,0:T(8,128)} %constant_dynamic-slice_fusion.8), channel_id=1, source_target_pairs={{0,16},{1,17},{2,18},{3,19},{4,12},{5,13},{6,14},{7,15},{8,24},{9,... | collective-permute-start | bytes 4718600 | tf_op jit(solution)/shard_map/ppermute | solution.py:280
  234.1 3.2 copy-start.1
  237.3 83.0 %all-to-all-start.2 = ((f32[8,128,384]{2,1,0:T(8,128)}), f32[8,128,384]{2,1,0:T(8,128)S(1)}, u32[]{:S(2)}, u32[]{:S(2)}) async-start(f32[8,128,384]{2,1,0:T(8,128)} %bitcast.52), calls=%async_computation.2 | async-start | bytes 3145728 | tf_op jit(solution)/shard_map/all_to_all | solution.py:248
  246.5 63.9 %copy-start.5 = (f32[768,1024]{1,0:T(8,128)S(1)}, f32[768,1024]{1,0:T(8,128)}, u32[]{:S(2)}) copy-start(f32[768,1024]{1,0:T(8,128)} %copy-done.4) | copy-start | bytes 9437188
  310.3 7.9 %copy-start.2 = (f32[1024,1024]{1,0:T(8,128)}, f32[1024,1024]{1,0:T(8,128)S(1)}, u32[]{:S(2)}) copy-start(f32[1024,1024]{1,0:T(8,128)S(1)} %inverse_factor.1) | copy-start | bytes 12582916
  318.3 5.6 copy-start.9
  318.3 30.4 %collective-permute-start.14 = (f32[384,1024]{1,0:T(8,128)S(1)}, f32[384,1024]{1,0:T(8,128)}, u32[]{:S(2)}, u32[]{:S(2)}) collective-permute-start(f32[384,1024]{1,0:T(8,128)S(1)} %fusion.14), channel_id=1, source_target_pairs={{0,16},{4,12},{8,24},{12,4},{16,0},{20,28},{24,8},{28,20},{1,17},{... | collective-permute-start | bytes 4718600 | tf_op jit(solution)/shard_map/ppermute | solution.py:292
  323.9 33.7 %all-to-all-start.3 = ((f32[8,128,384]{2,1,0:T(8,128)}), f32[8,128,384]{2,1,0:T(8,128)}, u32[]{:S(2)}, u32[]{:S(2)}) async-start(f32[8,128,384]{2,1,0:T(8,128)} %bitcast.13), calls=%async_computation.3 | async-start | bytes 3145728 | tf_op jit(solution)/shard_map/all_to_all | solution.py:250
  352.3 61.4 %collective-permute-start.15 = (f32[768,1024]{1,0:T(8,128)S(1)}, f32[768,1024]{1,0:T(8,128)}, u32[]{:S(2)}, u32[]{:S(2)}) collective-permute-start(f32[768,1024]{1,0:T(8,128)S(1)} %maximum_select_fusion.3), channel_id=1, source_target_pairs={{0,8},{4,20},{8,0},{12,28},{16,24},{20,4},{24,16},{28,12},{1,9},{5... | collective-permute-start | bytes 9437192 | tf_op jit(solution)/shard_map/ppermute | solution.py:292
  357.6 82.8 %all-to-all-start.1 = ((f32[8,48,3072]{2,1,0:T(8,128)}), f32[8,48,3072]{2,1,0:T(8,128)}, u32[]{:S(2)}, u32[]{:S(2)}) async-start(f32[8,48,3072]{2,1,0:T(8,128)} %bitcast.61), calls=%async_computation.1 | async-start | bytes 9437184 | tf_op jit(solution)/shard_map/all_to_all | solution.py:244
  364.0 56.2 %copy-start.13 = (s32[32]{0:T(128)S(1)}, s32[32]{0:T(128)}, u32[]{:S(2)}) copy-start(s32[32]{0:T(128)} %param.5) | copy-start | bytes 388
  419.1 136.9 %collective-permute-start.16 = (f32[1536,1024]{1,0:T(8,128)}, f32[1536,1024]{1,0:T(8,128)}, u32[]{:S(2)}, u32[]{:S(2)}) collective-permute-start(f32[1536,1024]{1,0:T(8,128)} %maximum_select_fusion.1), channel_id=1, source_target_pairs={{0,4},{4,0},{8,12},{12,8},{16,20},{20,16},{24,28},{28,24},{1,5},{5... | collective-permute-start | bytes 18874376 | tf_op jit(solution)/shard_map/ppermute | solution.py:272
  449.4 2.6 copy-start
  449.5 0.8 collective-permute-start.17
  452.0 93.6 %collective-permute-start.18 = (f32[512,1024]{1,0:T(8,128)S(1)}, f32[512,1024]{1,0:T(8,128)}, u32[]{:S(2)}, u32[]{:S(2)}) collective-permute-start(f32[512,1024]{1,0:T(8,128)S(1)} %broadcast_select_fusion), channel_id=1, source_target_pairs={{0,1},{2,3},{4,5},{6,7},{8,9},{10,11},{12,13},{14,15},{16,17},{18,... | collective-permute-start | bytes 6291464 | tf_op jit(solution)/shard_map/ppermute | solution.py:301
  545.6 20.9 %slice-start = ((s8[6291456]{0:T(1024)(128)(4,1)}), s8[4194304]{0:T(1024)(128)(4,1)S(1)}, s32[]{:S(2)}) async-start(s8[6291456]{0:T(1024)(128)(4,1)} %bitcast.53), calls=%async_computation.4 | async-start | bytes 8388608
  556.0 10.5 %slice-start.1 = ((s8[6291456]{0:T(1024)(128)(4,1)}), s8[2097152]{0:T(1024)(128)(4,1)S(1)}, s32[]{:S(2)}) async-start(s8[6291456]{0:T(1024)(128)(4,1)} %bitcast.53), calls=%async_computation.5 | async-start | bytes 4194304
  556.0 10.5 %copy-start.8 = (f32[512,1024]{1,0:T(8,128)S(1)}, f32[512,1024]{1,0:T(8,128)}, u32[]{:S(2)}) copy-start(f32[512,1024]{1,0:T(8,128)} %fusion.11) | copy-start | bytes 6291460
